TPU v7x, 32 devices: a whole 2x2x4 slice. The times are simulated.
32 devices in a mesh: row: 4 (over x, core), col: 8 (over z, y).
Axes of the slice: x: 2, y: 2, z: 4, core: 2. Of those that a mesh axis runs over, the one named last changes fastest.
Arguments:
- inputs: bfloat16 [512, 12288], P('col', 'row'), may hold values from -6 to 6
- weight: bfloat16 [12288, 24576], P('row', 'col'), may hold values from -0.0546875 to 0.0546875
- grad_out: bfloat16 [512, 24576], P('row', 'col'), may hold values from -1.2578125 to 1.2578125
Outputs:
- grad_input: bfloat16 [512, 12288], P('col', 'row')
- grad_weight: bfloat16 [12288, 24576], P('row', 'col')
All inputs are finite; a program needn't handle non-finite values.
Results may differ from a plain program's by a relative error of at most 0.02.
Values may be sent and summed in bfloat16 or wider, within the bound.
A program may use at most 128 MiB of HBM per device.

v0:
```python
import jax
import jax.numpy as jnp
from jax import lax
from jax.sharding import PartitionSpec as P


def gelu_slope(value):
    coef = 0.7978845608
    inner = coef * (value + 0.044715 * value * value * value)
    tanh_val = jnp.tanh(inner)
    return 0.5 * (1.0 + tanh_val) + 0.5 * value * (1.0 - tanh_val * tanh_val) * coef * (
        1.0 + 3.0 * 0.044715 * value * value
    )


def shards(inputs, weight, grad_out):
    gathered = lax.all_gather(inputs, "col", axis=0, tiled=True)
    partial_term = jnp.dot(gathered, weight, preferred_element_type=jnp.float32)
    pre_own = lax.psum_scatter(
        partial_term.astype(jnp.bfloat16), "row", scatter_dimension=0, tiled=True
    ).astype(jnp.float32)
    grad_own = (grad_out.astype(jnp.float32) * gelu_slope(pre_own)).astype(jnp.bfloat16)
    grad_pre = lax.all_gather(grad_own, "row", axis=0, tiled=True)
    grad_weight = lax.dot_general(
        gathered, grad_pre, (((0,), (0,)), ((), ())), preferred_element_type=jnp.float32
    )
    grad_input = lax.psum_scatter(
        lax.dot_general(
            grad_pre, weight, (((1,), (1,)), ((), ())), preferred_element_type=jnp.float32
        ).astype(jnp.bfloat16),
        "col",
        scatter_dimension=0,
        tiled=True,
    )
    return (grad_input, grad_weight.astype(jnp.bfloat16))


def solution(mesh):
    placed = (P("col", "row"), P("row", "col"), P("row", "col"))
    return jax.shard_map(
        shards,
        mesh=mesh,
        in_specs=placed,
        out_specs=(P("col", "row"), P("row", "col")),
        check_vma=False,
    )
```

profile of v0, /device:TPU:0, one launch (start us, length us, event | category | flops | bytes accessed | tf_op | source)
XLA Modules:
  0.0 254.8 jit_solution(11303025076899431536)
XLA Ops:
  7.2 0.0 all-gather.3.cloned.1.call-start
  7.2 0.7 all-gather.3.cloned.1.call-update
  7.9 0.0 reduce-scatter.3.cloned.1.call-start
  7.9 65.4 %all-gather.3.cloned.1.call-done = bf16[512,3072]{1,0:T(8,128)(2,1)} async-done(((bf16[64,3072]{1,0:T(8,128)(2,1)}), bf16[512,3072]{1,0:T(8,128)(2,1)}) %all-gather.3.cloned.1.call-update) | async-done | bytes 3145744 | tf_op jit(solution)/shard_map/all_gather | solution.py:17
  73.4 15.8 %convolution_convert_fusion.1 = bf16[512,3072]{1,0:T(8,128)(2,1)} fusion(bf16[512,3072]{1,0:T(8,128)(2,1)} %all-gather.3.cloned.1.call-done, bf16[3072,3072]{1,0:T(8,128)(2,1)} %param.4), kind=kOutput, calls=%fused_computation.2 | convolution fusion | flops 9665249280 | bytes 25165824 | tf_op jit(solution)/shard_map/dot_general | solution.py:18
  89.2 0.0 copy-start
  89.2 0.0 reduce-scatter.3.cloned.1.call-update
  89.2 0.0 all-gather.5.cloned.1.call-start
  89.2 36.7 %reduce-scatter.3.cloned.1.call-done = bf16[128,3072]{1,0:T(8,128)(2,1)} async-done(((bf16[512,3072]{1,0:T(8,128)(2,1)}), bf16[128,3072]{1,0:T(8,128)(2,1)}) %reduce-scatter.3.cloned.1.call-update) | async-done | bytes 786448 | tf_op jit(solution)/shard_map/reduce_scatter | solution.py:19
  125.9 0.0 copy-done
  125.9 3.1 %fusion.7 = bf16[128,3072]{1,0:T(8,128)(2,1)} fusion(bf16[128,3072]{1,0:T(8,128)(2,1)} %reduce-scatter.3.cloned.1.call-done, bf16[128,3072]{1,0:T(8,128)(2,1)S(1)} %copy-done), kind=kLoop, calls=%fused_computation.17 | loop fusion | flops 8257536 | bytes 2359296 | tf_op jit(solution)/shard_map/convert_element_type | solution.py:22
  129.0 0.0 all-gather.5.cloned.1.call-update
  129.1 0.2 reduce-scatter.5.cloned.1.call-start
  129.3 28.4 %all-gather.5.cloned.1.call-done = bf16[512,3072]{1,0:T(8,128)(2,1)} async-done(((bf16[128,3072]{1,0:T(8,128)(2,1)}), bf16[512,3072]{1,0:T(8,128)(2,1)}) %all-gather.5.cloned.1.call-update) | async-done | bytes 3145744 | tf_op jit(solution)/shard_map/all_gather | solution.py:23
  157.7 16.0 %convolution_convert_fusion = bf16[512,3072]{1,0:T(8,128)(2,1)} fusion(bf16[512,3072]{1,0:T(8,128)(2,1)} %all-gather.5.cloned.1.call-done, bf16[3072,3072]{1,0:T(8,128)(2,1)} %param.4), kind=kOutput, calls=%fused_computation.1 | convolution fusion | flops 9665249280 | bytes 25165824 | tf_op jit(solution)/shard_map/dot_general | solution.py:28
  173.8 0.0 copy-start.1
  173.8 0.0 reduce-scatter.5.cloned.1.call-update
  173.8 1.9 copy-done.1
  175.6 15.0 %convert_bitcast_fusion = bf16[3072,3072]{0,1:T(8,128)(2,1)} fusion(bf16[512,3072]{1,0:T(8,128)(2,1)} %all-gather.5.cloned.1.call-done, bf16[512,3072]{1,0:T(8,128)(2,1)S(1)} %copy-done.1), kind=kOutput, calls=%fused_computation | convolution fusion | flops 9673113600 | bytes 25165824 | tf_op jit(solution)/shard_map/dot_general | solution.py:24
  190.7 24.7 %copy.5 = bf16[3072,3072]{1,0:T(8,128)(2,1)} copy(bf16[3072,3072]{0,1:T(8,128)(2,1)} %convert_bitcast_fusion) | data formatting | bytes 37748736
  215.4 32.9 %reduce-scatter.5.cloned.1.call-done = bf16[64,3072]{1,0:T(8,128)(2,1)} async-done(((bf16[512,3072]{1,0:T(8,128)(2,1)}), bf16[64,3072]{1,0:T(8,128)(2,1)}) %reduce-scatter.5.cloned.1.call-update) | async-done | bytes 393232 | tf_op jit(solution)/shard_map/reduce_scatter | solution.py:27
Async XLA Ops:
  7.2 66.2 %all-gather.3.cloned.1.call-start = ((), (), s32[]{:S(2)}) async-start(), calls=%async_computation.2 | async-start | bytes 3538944 | tf_op jit(solution)/shard_map/all_gather | solution.py:17
  7.9 118.0 %reduce-scatter.3.cloned.1.call-start = ((), (), s32[]{:S(2)}) async-start(), calls=%async_computation.3 | async-start | bytes 3932160 | tf_op jit(solution)/shard_map/reduce_scatter | solution.py:19
  89.2 36.8 %copy-start = (bf16[128,3072]{1,0:T(8,128)(2,1)S(1)}, bf16[128,3072]{1,0:T(8,128)(2,1)}, u32[]{:S(2)}) copy-start(bf16[128,3072]{1,0:T(8,128)(2,1)} %param.5) | copy-start | bytes 2359300
  89.2 68.6 %all-gather.5.cloned.1.call-start = ((), (), s32[]{:S(2)}) async-start(), calls=%async_computation.4 | async-start | bytes 3932160 | tf_op jit(solution)/shard_map/all_gather | solution.py:23
  129.1 119.2 %reduce-scatter.5.cloned.1.call-start = ((), (), s32[]{:S(2)}) async-start(), calls=%async_computation.5 | async-start | bytes 3538944 | tf_op jit(solution)/shard_map/reduce_scatter | solution.py:27
  173.8 1.9 copy-start.1
Sparse Core Ops, SparseCore 0:
  10.2 63.1 all-gather.2
  89.3 36.5 reduce-scatter.2
  129.2 28.5 all-gather.4
  173.9 74.3 reduce-scatter.4
where the time goes:
time: 256 us; the launch traced here: 255 us
  waiting for transfers between devices  164 us (64%)
  matrix products  46.8 us (18%)
  local copies, waits for them, and re-layouts  26.6 us (10%)
  between operations  13.8 us (5%)
  other arithmetic  3.1 us (1%)
    all_gather x1, waiting for transfers between devices, shards(): gathered = lax.all_gather(inputs, 'col', axis=0, tiled=True)  65.4 us
    reduce_scatter x1, waiting for transfers between devices, shards(): lax.psum_scatter(partial_term.astype(jnp.bfloat16), 'row', scatter_dimens...  36.7 us
    reduce_scatter x1, waiting for transfers between devices, shards(): lax.psum_scatter(lax.dot_general(grad_pre, weight, (((1,), (1,)), ((), ()...  32.9 us
    all_gather x1, waiting for transfers between devices, shards(): grad_pre = lax.all_gather(grad_own, 'row', axis=0, tiled=True)  28.4 us
    unnamed x5, local copies, waits for them, and re-layouts  26.6 us
    dot_general x1, matrix products, shards(): lax.dot_general(grad_pre, weight, (((1,), (1,)), ((), ())), preferred_ele...  16 us
    dot_general x1, matrix products, shards(): partial_term = jnp.dot(gathered, weight, preferred_element_type=jnp.float32)  15.8 us
    dot_general x1, matrix products, shards(): lax.dot_general(gathered, grad_pre, (((0,), (0,)), ((), ())), preferred_e...  15 us
  transfers between devices with their start and end apart: 4, of which 4 were waited for; matrix products, arithmetic and copies ran while one was open for 16% of the time, Pallas kernels for 0%

commit v1 on v0

v1 whole, which is shorter than its diff:
```python
import functools

import jax
import jax.numpy as jnp
from jax import lax
from jax.experimental import pallas as pl
from jax.experimental.pallas import tpu as pltpu
from jax.sharding import PartitionSpec as P

MESH = pl.DeviceIdType.MESH
PAIR = 2


def gelu_slope(value):
    coef = 0.7978845608
    inner = coef * (value + 0.044715 * value * value * value)
    tanh_val = jnp.tanh(inner)
    return 0.5 * (1.0 + tanh_val) + 0.5 * value * (1.0 - tanh_val * tanh_val) * coef * (
        1.0 + 3.0 * 0.044715 * value * value
    )


def tile_of(width, most):
    tile = 128
    for size in range(128, most + 1, 128):
        if width % size == 0:
            tile = size
    return tile


def block(index, size):
    return pl.ds(pl.multiple_of(index * size, size), size)


def kernel(
    n_row, n_col,
    x_ref, w_ref, go_ref,
    gi_ref, x_out, gp_out,
    w, xs_all, go_all, part, core_in, chip, chip_in, gp, term, pair_in, both, line_in,
    w_sem, x_sem, go_sem, out_sem,
    ag_recv, ag_send, go_recv, go_send, core_recv, core_send, chip_recv, chip_send,
    gp_recv, gp_send, pair_recv, pair_send, line_recv, line_send,
):
    own, depth = x_ref.shape
    units = w_ref.shape[1]
    half = units // PAIR
    line = n_col // PAIR
    chips = n_row // PAIR
    rows = own * PAIR
    held = go_ref.shape[0]
    row, col = lax.axis_index("row"), lax.axis_index("col")
    at, side = col // PAIR, lax.rem(col, PAIR)
    across, core = row // PAIR, lax.rem(row, PAIR)
    mate = (across * PAIR + 1 - core, col)
    twin = (row, at * PAIR + 1 - side)

    def on_line(place):
        return (row, place * PAIR + side)

    def on_chip(place):
        return (place * PAIR + core, col)

    def remote(src, dst, send, recv, device):
        return pltpu.make_async_remote_copy(
            src_ref=src, dst_ref=dst, send_sem=send, recv_sem=recv,
            device_id=device, device_id_type=MESH,
        )

    def chunk_of(k):
        low = jnp.minimum(at, line - 1 - at)
        near = jnp.where(lax.rem(k, 2) == 1, at + (k + 1) // 2, at - (k + 1) // 2)
        far = jnp.where(at < line - 1 - at, at + (k - low), at - (k - low))
        return jnp.where(k <= 2 * low, near, far)

    def slot(q, s):
        return xs_all.at[block(q * PAIR + s, own), :]

    def own_to(which, device):
        return remote(x_ref, slot(at, side), ag_send.at[which, at], ag_recv.at[at, side], device)

    def to_twin(q):
        return remote(slot(q, side), slot(q, side), ag_send.at[0, q], ag_recv.at[q, side], twin)

    def onward(q):
        place = jnp.where(q < at, at + 1, at - 1)
        place = jnp.clip(place, 0, line - 1)
        return remote(slot(q, side), slot(q, side), ag_send.at[1, q], ag_recv.at[q, side], on_line(place))

    def goes_on(q):
        return ((q < at) & (at + 1 < line)) | ((q > at) & (at > 0))

    def arrived(q, s):
        return remote(slot(q, s), slot(q, s), ag_send.at[0, q], ag_recv.at[q, s], twin)

    def go_copy(step):
        other = lax.rem(row + step, n_row)
        return remote(
            go_ref.at[:, block(lax.rem(other, PAIR), half)],
            go_all.at[block(row, held), :],
            go_send.at[step - 1], go_recv.at[row], (other, col),
        )

    def go_arrived(source):
        view = go_all.at[block(source, held), :]
        return remote(view, view, go_send.at[0], go_recv.at[source], mate)

    def core_copy(q):
        return remote(
            part.at[q, :, block(1 - core, half)], core_in.at[q],
            core_send.at[q], core_recv.at[q], mate,
        )

    def chip_copy(q, step):
        place = lax.rem(across + step, chips)
        return remote(
            chip.at[q], chip_in.at[q, across],
            chip_send.at[q, step - 1], chip_recv.at[q, across], on_chip(place),
        )

    def chip_arrived(q, source):
        view = chip_in.at[q, source]
        return remote(view, view, chip_send.at[q, 0], chip_recv.at[q, source], mate)

    def gp_copy(q, which):
        view = gp.at[block(q, rows), block(which, half)]
        return remote(view, view, gp_send.at[q], gp_recv.at[q], mate)

    def pair_copy(q):
        return remote(
            term.at[q, block(1 - side, own), :], pair_in.at[q],
            pair_send.at[q], pair_recv.at[q], twin,
        )

    def line_copy(q):
        return remote(
            both.at[q], line_in.at[at], line_send.at[q], line_recv.at[at], on_line(q)
        )

    def line_arrived(source):
        view = line_in.at[source]
        return remote(view, view, line_send.at[source], line_recv.at[source], twin)

    w_copy = pltpu.make_async_copy(w_ref, w, w_sem)
    x_copy = pltpu.make_async_copy(x_ref, slot(at, side), x_sem)
    go_own = pltpu.make_async_copy(
        go_ref.at[:, block(core, half)], go_all.at[block(row, held), :], go_sem
    )
    w_copy.start()
    x_copy.start()
    go_own.start()

    barrier = pltpu.get_barrier_semaphore()
    pl.semaphore_signal(barrier, inc=1, device_id=twin, device_id_type=MESH)

    @pl.loop(1, line)
    def _(step):
        pl.semaphore_signal(
            barrier, inc=1, device_id=on_line(lax.rem(at + step, line)), device_id_type=MESH
        )

    @pl.loop(1, n_row)
    def _(step):
        pl.semaphore_signal(
            barrier, inc=1, device_id=(lax.rem(row + step, n_row), col), device_id_type=MESH
        )

    pl.semaphore_wait(barrier, line + n_row - 1)

    up, down = jnp.minimum(at + 1, line - 1), jnp.maximum(at - 1, 0)
    own_to(0, twin).start()

    @pl.when(at + 1 < line)
    def _():
        own_to(1, on_line(up)).start()

    @pl.when(at > 0)
    def _():
        own_to(2, on_line(down)).start()

    @pl.loop(1, n_row)
    def _(step):
        go_copy(step).start()

    go_own.wait()

    @pl.loop(1, n_row)
    def _(step):
        go_arrived(lax.rem(row + step, n_row)).wait_recv()

    x_copy.wait()
    w_copy.wait()

    tile = tile_of(half, 512)
    tiles = half // tile
    wide = tile_of(depth, 512)

    def first_product(q, which):
        @pl.loop(0, tiles)
        def _(j):
            columns = block(which * tiles + j, tile)
            part[q, :, columns] = jnp.dot(
                xs_all[block(q, rows), :], w[:, columns], preferred_element_type=jnp.float32
            ).astype(part.dtype)

    small = 16
    span = tile_of(half, 512)

    def slabs(height, width, step, body):
        across_tiles = width // step

        @pl.loop(0, (height // small) * across_tiles)
        def _(i):
            body(lax.div(i, across_tiles) * small, block(lax.rem(i, across_tiles), step))

    @pl.loop(0, line + 2)
    def _(k):
        q = chunk_of(jnp.minimum(k, line - 1))
        before = chunk_of(jnp.clip(k - 1, 0, line - 1))
        earlier = chunk_of(jnp.clip(k - 2, 0, line - 1))

        @pl.when(k + 1 < line)
        def _():
            coming = chunk_of(k + 1)
            arrived(coming, side).wait_recv()
            to_twin(coming).start()

            @pl.when(goes_on(coming))
            def _():
                onward(coming).start()

        @pl.when(k < line)
        def _():
            arrived(q, 1 - side).wait_recv()
            pltpu.make_async_copy(
                xs_all.at[block(q, rows), :], x_out.at[block(q, rows), :], out_sem.at[0, q]
            ).start()
            first_product(q, 1 - core)
            core_copy(q).start()
            first_product(q, core)
            core_copy(q).wait_recv()

            def add(top, columns):
                at_rows = pl.ds(pl.multiple_of(top, small), small)
                mine = part[q, at_rows, pl.ds(pl.multiple_of(core * half, half) + columns.start, span)]
                chip[q, at_rows, columns] = (
                    mine.astype(jnp.float32) + core_in[q, at_rows, columns].astype(jnp.float32)
                ).astype(chip.dtype)

            slabs(rows, half, span, add)

            @pl.loop(1, chips)
            def _(step):
                chip_copy(q, step).start()

        @pl.when((k >= 1) & (k <= line))
        def _():
            @pl.loop(1, chips)
            def _(step):
                chip_arrived(before, lax.rem(across + step, chips)).wait_recv()

            def slope(top, columns):
                at_rows = pl.ds(pl.multiple_of(top, small), small)
                total = chip[before, at_rows, columns].astype(jnp.float32)
                for step in range(1, chips):
                    source = lax.rem(across + step, chips)
                    total = total + chip_in[before, source, at_rows, columns].astype(jnp.float32)
                token = pl.ds(pl.multiple_of(before * rows + top, small), small)
                gp[token, pl.ds(pl.multiple_of(core * half, half) + columns.start, span)] = (
                    go_all[token, columns].astype(jnp.float32) * gelu_slope(total)
                ).astype(gp.dtype)

            slabs(rows, half, span, slope)
            gp_copy(before, core).start()
            gp_copy(before, 1 - core).wait_recv()
            pltpu.make_async_copy(
                gp.at[block(before, rows), :], gp_out.at[block(before, rows), :], out_sem.at[1, before]
            ).start()

            @pl.loop(0, depth // wide)
            def _(j):
                columns = block(j, wide)
                term[before, :, columns] = lax.dot_general(
                    gp[block(before, rows), :], w[columns, :], (((1,), (1,)), ((), ())),
                    preferred_element_type=jnp.float32,
                ).astype(term.dtype)

            pair_copy(before).start()

        @pl.when(k >= 2)
        def _():
            pair_copy(earlier).wait_recv()

            def add(top, columns):
                at_rows = pl.ds(pl.multiple_of(top, small), small)
                mine = term[earlier, pl.ds(pl.multiple_of(side * own + top, small), small), columns]
                both[earlier, at_rows, columns] = (
                    mine.astype(jnp.float32) + pair_in[earlier, at_rows, columns].astype(jnp.float32)
                ).astype(both.dtype)

            slabs(own, depth, wide, add)

            @pl.when(earlier != at)
            def _():
                line_copy(earlier).start()

    @pl.loop(1, line)
    def _(step):
        line_arrived(lax.rem(at + step, line)).wait_recv()

    def finish(top, columns):
        at_rows = pl.ds(pl.multiple_of(top, small), small)
        total = both[at, at_rows, columns].astype(jnp.float32)
        for step in range(1, line):
            total = total + line_in[lax.rem(at + step, line), at_rows, columns].astype(jnp.float32)
        gi_ref[at_rows, columns] = total.astype(gi_ref.dtype)

    slabs(own, depth, wide, finish)

    own_to(0, twin).wait_send()

    @pl.when(at + 1 < line)
    def _():
        own_to(1, on_line(up)).wait_send()

    @pl.when(at > 0)
    def _():
        own_to(2, on_line(down)).wait_send()

    @pl.loop(1, n_row)
    def _(step):
        go_copy(step).wait_send()

    @pl.loop(0, line)
    def _(q):
        @pl.when(q != at)
        def _():
            to_twin(q).wait_send()
            line_copy(q).wait_send()

        @pl.when(goes_on(q))
        def _():
            onward(q).wait_send()

        core_copy(q).wait_send()

        @pl.loop(1, chips)
        def _(step):
            chip_copy(q, step).wait_send()

        gp_copy(q, core).wait_send()
        pair_copy(q).wait_send()
        pltpu.make_async_copy(
            xs_all.at[block(q, rows), :], x_out.at[block(q, rows), :], out_sem.at[0, q]
        ).wait()
        pltpu.make_async_copy(
            gp.at[block(q, rows), :], gp_out.at[block(q, rows), :], out_sem.at[1, q]
        ).wait()


def fused(n_row, n_col, inputs, weight, grad_out):
    own, depth = inputs.shape
    units = weight.shape[1]
    half = units // PAIR
    line, chips = n_col // PAIR, n_row // PAIR
    rows, tokens = own * PAIR, own * n_col
    held = grad_out.shape[0]
    bf16 = jnp.bfloat16
    DMA = pltpu.SemaphoreType.DMA
    flops = 4 * tokens * depth * units
    return pl.pallas_call(
        functools.partial(kernel, n_row, n_col),
        out_shape=(
            jax.ShapeDtypeStruct((own, depth), bf16),
            jax.ShapeDtypeStruct((tokens, depth), bf16),
            jax.ShapeDtypeStruct((tokens, units), bf16),
        ),
        in_specs=[pl.BlockSpec(memory_space=pl.ANY)] * 3,
        out_specs=(
            pl.BlockSpec(memory_space=pltpu.VMEM),
            pl.BlockSpec(memory_space=pl.ANY),
            pl.BlockSpec(memory_space=pl.ANY),
        ),
        scratch_shapes=[
            pltpu.VMEM((depth, units), bf16),
            pltpu.VMEM((tokens, depth), bf16),
            pltpu.VMEM((held * n_row, half), bf16),
            pltpu.VMEM((line, rows, units), bf16),
            pltpu.VMEM((line, rows, half), bf16),
            pltpu.VMEM((line, rows, half), bf16),
            pltpu.VMEM((line, chips, rows, half), bf16),
            pltpu.VMEM((tokens, units), bf16),
            pltpu.VMEM((line, rows, depth), bf16),
            pltpu.VMEM((line, own, depth), bf16),
            pltpu.VMEM((line, own, depth), bf16),
            pltpu.VMEM((line, own, depth), bf16),
            DMA, DMA, DMA, DMA((2, line)),
            DMA((line, PAIR)), DMA((3, line)),
            DMA((n_row,)), DMA((n_row,)),
            DMA((line,)), DMA((line,)),
            DMA((line, chips)), DMA((line, chips)),
            DMA((line,)), DMA((line,)),
            DMA((line,)), DMA((line,)),
            DMA((line,)), DMA((line,)),
        ],
        cost_estimate=pl.CostEstimate(
            flops=flops, bytes_accessed=2 * depth * units, transcendentals=tokens * half
        ),
        compiler_params=pltpu.CompilerParams(
            collective_id=0, has_side_effects=True, vmem_limit_bytes=58 * 1024 * 1024
        ),
    )(inputs, weight, grad_out)


def solution(mesh):
    n_row, n_col = mesh.shape["row"], mesh.shape["col"]

    def shards(inputs, weight, grad_out):
        grad_input, gathered, grad_pre = fused(n_row, n_col, inputs, weight, grad_out)
        grad_weight = lax.dot_general(
            gathered, grad_pre, (((0,), (0,)), ((), ())), preferred_element_type=jnp.float32
        )
        return grad_input, grad_weight.astype(jnp.bfloat16)

    return jax.shard_map(
        shards,
        mesh=mesh,
        in_specs=(P("col", "row"), P("row", "col"), P("row", "col")),
        out_specs=(P("col", "row"), P("row", "col")),
        check_vma=False,
    )
```

time: 256 us -> 147 us (0.57)
  waiting for transfers between devices: 164 us -> 0 us
  Pallas kernels: 0 us -> 129 us
  matrix products: 46.8 us -> 16.4 us
  local copies, waits for them, and re-layouts: 26.6 us -> 0.75 us
  between operations: 13.8 us -> 0.65 us
  other arithmetic: 3.1 us -> 0 us
    pallas_call x0 -> x1, Pallas kernels: none -> 129 us  [fused(): pl.pallas_call(functools.partial(kernel, n_row, n_col), out_shape=(jax.Sh...]
    all_gather x2 -> x0, waiting for transfers between devices: 93.9 us -> none  [the longest x1 65.4 us: shards(): gathered = lax.all_gather(inputs, 'col', axis=0, tiled=True)]
    reduce_scatter x2 -> x0, waiting for transfers between devices: 69.6 us -> none  [the longest x1 36.7 us: shards(): lax.psum_scatter(partial_term.astype(jnp.bfloat16), 'row', scatter_dimens...]
    dot_general x2 -> x0, matrix products: 31.8 us -> none  [the longest x1 16 us: shards(): lax.dot_general(grad_pre, weight, (((1,), (1,)), ((), ())), preferred_ele...]
    unnamed x5 -> x3, local copies, waits for them, and re-layouts: 26.6 us -> 0.75 us
    convert_element_type x1 -> x0, other arithmetic: 3.1 us -> none  [shards(): (grad_out.astype(jnp.float32) * gelu_slope(pre_own)).astype(jnp.bfloat16)]
  transfers between devices with their start and end apart: 4 -> 0, of which waited for: 4 -> 0; matrix products, arithmetic and copies ran while one was open for 16% -> 0% of each run, Pallas kernels for 0% -> 0%
where the time goes in v1:
time: 147 us
  Pallas kernels  129 us (88%)
  matrix products  16.4 us (11%)
    pallas_call x1, Pallas kernels, fused(): pl.pallas_call(functools.partial(kernel, n_row, n_col), out_shape=(jax.Sh...  129 us
    dot_general x1, matrix products, shards(): lax.dot_general(gathered, grad_pre, (((0,), (0,)), ((), ())), preferred_e...  16.4 us

profile of v1, /device:TPU:0, one launch (start us, length us, event | category | flops | bytes accessed | tf_op | source)
XLA Modules:
  0.0 147.0 jit_solution(10812222098552400953)
XLA Ops:
  0.6 129.2 %shard_map.50 = (bf16[64,3072]{1,0:T(8,128)(2,1)}, bf16[512,3072]{1,0:T(8,128)(2,1)}, bf16[512,3072]{1,0:T(8,128)(2,1)}) custom-call(bf16[64,3072]{1,0:T(8,128)(2,1)} %x_ref.1, bf16[3072,3072]{1,0:T(8,128)(2,1)} %w_ref.1, bf16[128,3072]{1,0:T(8,128)(2,1)} %go_ref.1), custom_call_target="tpu_custom_call" | custom-call | flops 19327352832 | bytes 18874368 | tf_op jit(solution)/shard_map/pallas_call | solution.py:370
  129.9 0.0 copy-start
  129.9 16.4 %convolution_convert_fusion = bf16[3072,3072]{1,0:T(8,128)(2,1)} fusion(bf16[512,3072]{1,0:T(8,128)(2,1)} %get-tuple-element.6, bf16[512,3072]{1,0:T(8,128)(2,1)} %get-tuple-element.7), kind=kOutput, calls=%fused_computation | convolution fusion | flops 9673113600 | bytes 25165824 | tf_op jit(solution)/shard_map/dot_general | solution.py:419
  146.3 0.0 copy-done
  146.3 0.7 copy.6
Async XLA Ops:
  129.9 16.4 %copy-start = (bf16[64,3072]{1,0:T(8,128)(2,1)S(1)}, bf16[64,3072]{1,0:T(8,128)(2,1)}, u32[]{:S(2)}) copy-start(bf16[64,3072]{1,0:T(8,128)(2,1)} %get-tuple-element.10) | copy-start | bytes 1179652

commit v2 on v1

v2 whole, which is shorter than its diff:
```python
import functools

import jax
import jax.numpy as jnp
from jax import lax
from jax.experimental import pallas as pl
from jax.experimental.pallas import tpu as pltpu
from jax.sharding import PartitionSpec as P

MESH = pl.DeviceIdType.MESH
PAIR = 2
TILE = 512
WIDE = 768


def gelu_slope(value):
    coef = 0.7978845608
    inner = coef * (value + 0.044715 * value * value * value)
    tanh_val = jnp.tanh(inner)
    return 0.5 * (1.0 + tanh_val) + 0.5 * value * (1.0 - tanh_val * tanh_val) * coef * (
        1.0 + 3.0 * 0.044715 * value * value
    )


def tile_of(width, most):
    tile = 128
    for size in range(128, most + 1, 128):
        if width % size == 0:
            tile = size
    return tile


def block(index, size):
    return pl.ds(pl.multiple_of(index * size, size), size)


def kernel(
    n_row, n_col,
    x_ref, w_ref, go_ref,
    gi_ref, x_out, gp_out,
    w, xs_all, go_all, part, core_in, chip, chip_in, gp, term, pair_in, both, sib_in, summed, line_in,
    w_sem, x_sem, go_sem, out_sem,
    ag_recv, ag_send, go_recv, go_send, core_recv, core_send, chip_recv, chip_send,
    gp_recv, gp_send, pair_recv, pair_send, sib_recv, sib_send, line_recv, line_send,
):
    own, depth = x_ref.shape
    units = w_ref.shape[1]
    half = units // PAIR
    line = n_col // PAIR
    groups = line // PAIR
    chips = n_row // PAIR
    big = own * PAIR * PAIR
    held = go_ref.shape[0]
    tile, wide = tile_of(half, TILE), tile_of(depth, WIDE)
    tiles, pieces = half // tile, depth // wide
    small = 16
    row, col = lax.axis_index("row"), lax.axis_index("col")
    at, side = lax.div(col, PAIR), lax.rem(col, PAIR)
    group, sib = lax.div(at, PAIR), lax.rem(at, PAIR)
    across, core = lax.div(row, PAIR), lax.rem(row, PAIR)
    mate = (across * PAIR + 1 - core, col)
    twin = (row, at * PAIR + 1 - side)

    def on_line(place):
        return (row, place * PAIR + side)

    def on_chip(place):
        return (place * PAIR + core, col)

    sibling = on_line(group * PAIR + 1 - sib)

    def remote(src, dst, send, recv, device):
        return pltpu.make_async_remote_copy(
            src_ref=src, dst_ref=dst, send_sem=send, recv_sem=recv,
            device_id=device, device_id_type=MESH,
        )

    def group_of(k):
        low = jnp.minimum(group, groups - 1 - group)
        step = lax.div(k + 1, 2)
        near = jnp.where(lax.rem(k, 2) == 1, group + step, group - step)
        far = jnp.where(group < groups - 1 - group, group + (k - low), group - (k - low))
        return jnp.where(k <= 2 * low, near, far)

    def block_of(g, i):
        first = jnp.where(g == group, sib, jnp.where(g > group, 0, 1))
        return g * PAIR + (first if i == 0 else 1 - first)

    def slot(q, s):
        return xs_all.at[block(q * PAIR + s, own), :]

    def own_to(which, device):
        return remote(x_ref, slot(at, side), ag_send.at[which, at], ag_recv.at[at, side], device)

    def to_twin(q):
        return remote(slot(q, side), slot(q, side), ag_send.at[0, q], ag_recv.at[q, side], twin)

    def onward(q):
        place = jnp.clip(jnp.where(q < at, at + 1, at - 1), 0, line - 1)
        return remote(slot(q, side), slot(q, side), ag_send.at[1, q], ag_recv.at[q, side], on_line(place))

    def goes_on(q):
        return ((q < at) & (at + 1 < line)) | ((q > at) & (at > 0))

    def arrived(q, s):
        return remote(slot(q, s), slot(q, s), ag_send.at[0, q], ag_recv.at[q, s], twin)

    def forward(q):
        arrived(q, side).wait_recv()
        to_twin(q).start()

        @pl.when(goes_on(q))
        def _():
            onward(q).start()

    def go_copy(step):
        other = lax.rem(row + step, n_row)
        return remote(
            go_ref.at[:, block(lax.rem(other, PAIR), half)],
            go_all.at[block(row, held), :],
            go_send.at[step - 1], go_recv.at[row], (other, col),
        )

    def go_arrived(source):
        view = go_all.at[block(source, held), :]
        return remote(view, view, go_send.at[0], go_recv.at[source], mate)

    def core_copy(g, j):
        return remote(
            part.at[g, :, block((1 - core) * tiles + j, tile)], core_in.at[g, :, block(j, tile)],
            core_send.at[g, j], core_recv.at[g, j], mate,
        )

    def chip_copy(g, step, j):
        place = lax.rem(across + step, chips)
        return remote(
            chip.at[g, :, block(j, tile)], chip_in.at[g, across, :, block(j, tile)],
            chip_send.at[g, step - 1, j], chip_recv.at[g, across, j], on_chip(place),
        )

    def chip_arrived(g, source, j):
        view = chip_in.at[g, source, :, block(j, tile)]
        return remote(view, view, chip_send.at[g, 0, j], chip_recv.at[g, source, j], mate)

    def gp_copy(g, which, j):
        view = gp.at[block(g, big), block(which * tiles + j, tile)]
        return remote(view, view, gp_send.at[g, j], gp_recv.at[g, j], mate)

    def pair_copy(g, b, j):
        return remote(
            term.at[g, block(b * PAIR + 1 - side, own), block(j, wide)],
            pair_in.at[g, block(b, own), block(j, wide)],
            pair_send.at[g, b, j], pair_recv.at[g, b, j], twin,
        )

    def sib_copy(g, j):
        return remote(
            both.at[g, block(1 - sib, own), block(j, wide)], sib_in.at[g, :, block(j, wide)],
            sib_send.at[g, j], sib_recv.at[g, j], sibling,
        )

    def line_copy(g, j):
        return remote(
            summed.at[g, :, block(j, wide)], line_in.at[group, :, block(j, wide)],
            line_send.at[g, j], line_recv.at[group, j], on_line(g * PAIR + sib),
        )

    def line_arrived(source, j):
        view = line_in.at[source, :, block(j, wide)]
        return remote(view, view, line_send.at[source, j], line_recv.at[source, j], twin)

    def x_copy_out(g):
        return pltpu.make_async_copy(
            xs_all.at[block(g, big), :], x_out.at[block(g, big), :], out_sem.at[0, g]
        )

    def gp_copy_out(g):
        return pltpu.make_async_copy(
            gp.at[block(g, big), :], gp_out.at[block(g, big), :], out_sem.at[1, g]
        )

    w_copy = pltpu.make_async_copy(w_ref, w, w_sem)
    x_copy = pltpu.make_async_copy(x_ref, slot(at, side), x_sem)
    go_own = pltpu.make_async_copy(
        go_ref.at[:, block(core, half)], go_all.at[block(row, held), :], go_sem
    )
    x_copy.start()
    go_own.start()
    w_copy.start()

    barrier = pltpu.get_barrier_semaphore()
    pl.semaphore_signal(barrier, inc=1, device_id=twin, device_id_type=MESH)

    @pl.loop(1, line)
    def _(step):
        pl.semaphore_signal(
            barrier, inc=1, device_id=on_line(lax.rem(at + step, line)), device_id_type=MESH
        )

    @pl.loop(1, n_row)
    def _(step):
        pl.semaphore_signal(
            barrier, inc=1, device_id=(lax.rem(row + step, n_row), col), device_id_type=MESH
        )

    pl.semaphore_wait(barrier, line + n_row - 1)

    up, down = jnp.minimum(at + 1, line - 1), jnp.maximum(at - 1, 0)
    own_to(0, twin).start()

    @pl.when(at + 1 < line)
    def _():
        own_to(1, on_line(up)).start()

    @pl.when(at > 0)
    def _():
        own_to(2, on_line(down)).start()

    @pl.loop(1, n_row)
    def _(step):
        go_copy(step).start()

    x_copy.wait()
    forward(block_of(group, 1))

    def slabs(height, base, width, body):
        @pl.loop(0, height // small)
        def _(i):
            body(pl.multiple_of(i * small, small), pl.ds(pl.multiple_of(base * width, width), width))

    def at_row(start):
        return pl.ds(pl.multiple_of(start, small), small)

    def product(g, which):
        columns = block(which, tile)
        part[g, :, columns] = jnp.dot(
            xs_all[block(g, big), :], w[:, columns], preferred_element_type=jnp.float32
        ).astype(part.dtype)

    @pl.loop(0, groups + 3)
    def _(k):
        g = group_of(jnp.minimum(k, groups - 1))
        g1 = group_of(jnp.clip(k - 1, 0, groups - 1))
        g2 = group_of(jnp.clip(k - 2, 0, groups - 1))
        g3 = group_of(jnp.clip(k - 3, 0, groups - 1))
        coming = group_of(jnp.minimum(k + 1, groups - 1))
        more = k + 1 < groups
        second = block_of(coming, 1)

        @pl.when(more)
        def _():
            forward(block_of(coming, 0))

        @pl.when(k < groups)
        def _():
            for i in range(PAIR):
                arrived(block_of(g, i), 1 - side).wait_recv()
            x_copy_out(g).start()

            @pl.when(k == 0)
            def _():
                w_copy.wait()

            @pl.loop(0, tiles)
            def _(j):
                product(g, (1 - core) * tiles + j)
                core_copy(g, j).start()
                product(g, core * tiles + j)

                @pl.when(more & (j == tiles // 2) & goes_on(second))
                def _():
                    forward(second)

                core_copy(g, j).wait_recv()

                def add(top, columns):
                    mine = part[g, at_row(top), block(core * tiles + j, tile)]
                    chip[g, at_row(top), columns] = (
                        mine.astype(jnp.float32)
                        + core_in[g, at_row(top), columns].astype(jnp.float32)
                    ).astype(chip.dtype)

                slabs(big, j, tile, add)

                @pl.loop(1, chips)
                def _(step):
                    chip_copy(g, step, j).start()

            @pl.when(more & ~goes_on(second))
            def _():
                forward(second)

        @pl.when((k >= 1) & (k <= groups))
        def _():
            @pl.when(k == 1)
            def _():
                go_own.wait()

                @pl.loop(1, n_row)
                def _(step):
                    go_arrived(lax.rem(row + step, n_row)).wait_recv()

            @pl.loop(0, tiles)
            def _(j):
                @pl.loop(1, chips)
                def _(step):
                    chip_arrived(g1, lax.rem(across + step, chips), j).wait_recv()

                def slope(top, columns):
                    total = chip[g1, at_row(top), columns].astype(jnp.float32)
                    for step in range(1, chips):
                        source = lax.rem(across + step, chips)
                        total = total + chip_in[g1, source, at_row(top), columns].astype(jnp.float32)
                    token = at_row(g1 * big + top)
                    gp[token, block(core * tiles + j, tile)] = (
                        go_all[token, columns].astype(jnp.float32) * gelu_slope(total)
                    ).astype(gp.dtype)

                slabs(big, j, tile, slope)
                gp_copy(g1, core, j).start()

            @pl.loop(0, tiles)
            def _(j):
                gp_copy(g1, 1 - core, j).wait_recv()

            gp_copy_out(g1).start()

            @pl.loop(0, pieces)
            def _(j):
                columns = block(j, wide)
                term[g1, :, columns] = lax.dot_general(
                    gp[block(g1, big), :], w[columns, :], (((1,), (1,)), ((), ())),
                    preferred_element_type=jnp.float32,
                ).astype(term.dtype)
                for b in range(PAIR):
                    pair_copy(g1, b, j).start()

        @pl.when((k >= 2) & (k <= groups + 1))
        def _():
            @pl.loop(0, pieces)
            def _(j):
                for b in range(PAIR):
                    pair_copy(g2, b, j).wait_recv()

                    def add(top, columns):
                        mine = term[g2, at_row((b * PAIR + side) * own + top), columns]
                        here = at_row(b * own + top)
                        both[g2, here, columns] = (
                            mine.astype(jnp.float32)
                            + pair_in[g2, here, columns].astype(jnp.float32)
                        ).astype(both.dtype)

                    slabs(own, j, wide, add)
                sib_copy(g2, j).start()

        @pl.when(k >= 3)
        def _():
            @pl.loop(0, pieces)
            def _(j):
                sib_copy(g3, j).wait_recv()

                def add(top, columns):
                    mine = both[g3, at_row(sib * own + top), columns]
                    summed[g3, at_row(top), columns] = (
                        mine.astype(jnp.float32)
                        + sib_in[g3, at_row(top), columns].astype(jnp.float32)
                    ).astype(summed.dtype)

                slabs(own, j, wide, add)

                @pl.when(g3 != group)
                def _():
                    line_copy(g3, j).start()

    @pl.loop(0, pieces)
    def _(j):
        @pl.loop(1, groups)
        def _(step):
            line_arrived(lax.rem(group + step, groups), j).wait_recv()

        def finish(top, columns):
            total = summed[group, at_row(top), columns].astype(jnp.float32)
            for step in range(1, groups):
                source = lax.rem(group + step, groups)
                total = total + line_in[source, at_row(top), columns].astype(jnp.float32)
            gi_ref[at_row(top), columns] = total.astype(gi_ref.dtype)

        slabs(own, j, wide, finish)

    own_to(0, twin).wait_send()

    @pl.when(at + 1 < line)
    def _():
        own_to(1, on_line(up)).wait_send()

    @pl.when(at > 0)
    def _():
        own_to(2, on_line(down)).wait_send()

    @pl.loop(1, n_row)
    def _(step):
        go_copy(step).wait_send()

    @pl.loop(0, line)
    def _(q):
        @pl.when(q != at)
        def _():
            to_twin(q).wait_send()

        @pl.when(goes_on(q))
        def _():
            onward(q).wait_send()

    @pl.loop(0, groups)
    def _(g):
        @pl.loop(0, tiles)
        def _(j):
            core_copy(g, j).wait_send()

            @pl.loop(1, chips)
            def _(step):
                chip_copy(g, step, j).wait_send()

            gp_copy(g, core, j).wait_send()

        @pl.loop(0, pieces)
        def _(j):
            for b in range(PAIR):
                pair_copy(g, b, j).wait_send()
            sib_copy(g, j).wait_send()

            @pl.when(g != group)
            def _():
                line_copy(g, j).wait_send()

        x_copy_out(g).wait()
        gp_copy_out(g).wait()


def fused(n_row, n_col, inputs, weight, grad_out):
    own, depth = inputs.shape
    units = weight.shape[1]
    half = units // PAIR
    line, chips = n_col // PAIR, n_row // PAIR
    groups = line // PAIR
    big, tokens = own * PAIR * PAIR, own * n_col
    tiles, pieces = half // tile_of(half, TILE), depth // tile_of(depth, WIDE)
    held = grad_out.shape[0]
    bf16 = jnp.bfloat16
    DMA = pltpu.SemaphoreType.DMA
    flops = 4 * tokens * depth * units
    return pl.pallas_call(
        functools.partial(kernel, n_row, n_col),
        out_shape=(
            jax.ShapeDtypeStruct((own, depth), bf16),
            jax.ShapeDtypeStruct((tokens, depth), bf16),
            jax.ShapeDtypeStruct((tokens, units), bf16),
        ),
        in_specs=[pl.BlockSpec(memory_space=pl.ANY)] * 3,
        out_specs=(
            pl.BlockSpec(memory_space=pltpu.VMEM),
            pl.BlockSpec(memory_space=pl.ANY),
            pl.BlockSpec(memory_space=pl.ANY),
        ),
        scratch_shapes=[
            pltpu.VMEM((depth, units), bf16),
            pltpu.VMEM((tokens, depth), bf16),
            pltpu.VMEM((held * n_row, half), bf16),
            pltpu.VMEM((groups, big, units), bf16),
            pltpu.VMEM((groups, big, half), bf16),
            pltpu.VMEM((groups, big, half), bf16),
            pltpu.VMEM((groups, chips, big, half), bf16),
            pltpu.VMEM((tokens, units), bf16),
            pltpu.VMEM((groups, big, depth), bf16),
            pltpu.VMEM((groups, own * PAIR, depth), bf16),
            pltpu.VMEM((groups, own * PAIR, depth), bf16),
            pltpu.VMEM((groups, own, depth), bf16),
            pltpu.VMEM((groups, own, depth), bf16),
            pltpu.VMEM((groups, own, depth), bf16),
            DMA, DMA, DMA, DMA((2, groups)),
            DMA((line, PAIR)), DMA((3, line)),
            DMA((n_row,)), DMA((n_row,)),
            DMA((groups, tiles)), DMA((groups, tiles)),
            DMA((groups, chips, tiles)), DMA((groups, chips, tiles)),
            DMA((groups, tiles)), DMA((groups, tiles)),
            DMA((groups, PAIR, pieces)), DMA((groups, PAIR, pieces)),
            DMA((groups, pieces)), DMA((groups, pieces)),
            DMA((groups, pieces)), DMA((groups, pieces)),
        ],
        cost_estimate=pl.CostEstimate(
            flops=flops, bytes_accessed=2 * depth * units, transcendentals=tokens * half
        ),
        compiler_params=pltpu.CompilerParams(
            collective_id=0, has_side_effects=True, vmem_limit_bytes=58 * 1024 * 1024
        ),
    )(inputs, weight, grad_out)


def solution(mesh):
    n_row, n_col = mesh.shape["row"], mesh.shape["col"]

    def shards(inputs, weight, grad_out):
        grad_input, gathered, grad_pre = fused(n_row, n_col, inputs, weight, grad_out)
        grad_weight = lax.dot_general(
            gathered, grad_pre, (((0,), (0,)), ((), ())), preferred_element_type=jnp.float32
        )
        return grad_input, grad_weight.astype(jnp.bfloat16)

    return jax.shard_map(
        shards,
        mesh=mesh,
        in_specs=(P("col", "row"), P("row", "col"), P("row", "col")),
        out_specs=(P("col", "row"), P("row", "col")),
        check_vma=False,
    )
```

time: 147 us -> 135 us (0.918)
  Pallas kernels: 129 us -> 117 us
    pallas_call x1, Pallas kernels: 129 us -> 117 us  [fused(): pl.pallas_call(functools.partial(kernel, n_row, n_col), out_shape=(jax.Sh...]
where the time goes in v2:
time: 135 us
  Pallas kernels  117 us (87%)
  matrix products  16.4 us (12%)
    pallas_call x1, Pallas kernels, fused(): pl.pallas_call(functools.partial(kernel, n_row, n_col), out_shape=(jax.Sh...  117 us
    dot_general x1, matrix products, shards(): lax.dot_general(gathered, grad_pre, (((0,), (0,)), ((), ())), preferred_e...  16.4 us

profile of v2, /device:TPU:0, one launch (start us, length us, event | category | flops | bytes accessed | tf_op | source)
XLA Modules:
  0.0 134.6 jit_solution(8624664579191167062)
XLA Ops:
  0.6 116.8 %shard_map.50 = (bf16[64,3072]{1,0:T(8,128)(2,1)}, bf16[512,3072]{1,0:T(8,128)(2,1)}, bf16[512,3072]{1,0:T(8,128)(2,1)}) custom-call(bf16[64,3072]{1,0:T(8,128)(2,1)} %x_ref.1, bf16[3072,3072]{1,0:T(8,128)(2,1)} %w_ref.1, bf16[128,3072]{1,0:T(8,128)(2,1)} %go_ref.1), custom_call_target="tpu_custom_call" | custom-call | flops 19327352832 | bytes 18874368 | tf_op jit(solution)/shard_map/pallas_call | solution.py:452
  117.4 0.0 copy-start
  117.4 16.4 %convolution_convert_fusion = bf16[3072,3072]{1,0:T(8,128)(2,1)} fusion(bf16[512,3072]{1,0:T(8,128)(2,1)} %get-tuple-element.6, bf16[512,3072]{1,0:T(8,128)(2,1)} %get-tuple-element.7), kind=kOutput, calls=%fused_computation | convolution fusion | flops 9673113600 | bytes 25165824 | tf_op jit(solution)/shard_map/dot_general | solution.py:504
  133.9 0.0 copy-done
  133.9 0.7 copy.6
Async XLA Ops:
  117.4 16.4 %copy-start = (bf16[64,3072]{1,0:T(8,128)(2,1)S(1)}, bf16[64,3072]{1,0:T(8,128)(2,1)}, u32[]{:S(2)}) copy-start(bf16[64,3072]{1,0:T(8,128)(2,1)} %get-tuple-element.10) | copy-start | bytes 1179652

commit v3 on v2

--- a/solution.py
+++ b/solution.py
@@ -40,7 +40,7 @@
     gi_ref, x_out, gp_out,
     w, xs_all, go_all, part, core_in, chip, chip_in, gp, term, pair_in, both, sib_in, summed, line_in,
     w_sem, x_sem, go_sem, out_sem,
-    ag_recv, ag_send, go_recv, go_send, core_recv, core_send, chip_recv, chip_send,
+    z_recv, z_send, y_recv, y_send, go_recv, go_send, core_recv, core_send, chip_recv, chip_send,
     gp_recv, gp_send, pair_recv, pair_send, sib_recv, sib_send, line_recv, line_send,
 ):
     own, depth = x_ref.shape
@@ -67,7 +67,8 @@
     def on_chip(place):
         return (place * PAIR + core, col)
 
-    sibling = on_line(group * PAIR + 1 - sib)
+    beside = group * PAIR + 1 - sib
+    sibling = on_line(beside)
 
     def remote(src, dst, send, recv, device):
         return pltpu.make_async_remote_copy(
@@ -89,29 +90,39 @@
     def slot(q, s):
         return xs_all.at[block(q * PAIR + s, own), :]
 
+    def slot_half(q, s, h):
+        return xs_all.at[block((q * PAIR + s) * 2 + h, own // 2), :]
+
     def own_to(which, device):
-        return remote(x_ref, slot(at, side), ag_send.at[which, at], ag_recv.at[at, side], device)
-
-    def to_twin(q):
-        return remote(slot(q, side), slot(q, side), ag_send.at[0, q], ag_recv.at[q, side], twin)
+        return remote(x_ref, slot(at, side), z_send.at[which, at], z_recv.at[at], device)
+
+    def own_half(h):
+        return remote(
+            x_ref.at[block(h, own // 2), :], slot_half(at, side, h),
+            y_send.at[at, h], y_recv.at[at, h], twin,
+        )
+
+    def to_twin(q, h):
+        view = slot_half(q, side, h)
+        return remote(view, view, y_send.at[q, h], y_recv.at[q, h], twin)
+
+    def twin_to_sibling():
+        view = slot_half(at, 1 - side, 1)
+        return remote(view, view, y_send.at[beside, 1], y_recv.at[at, 1], sibling)
 
     def onward(q):
         place = jnp.clip(jnp.where(q < at, at + 1, at - 1), 0, line - 1)
-        return remote(slot(q, side), slot(q, side), ag_send.at[1, q], ag_recv.at[q, side], on_line(place))
+        return remote(slot(q, side), slot(q, side), z_send.at[1, q], z_recv.at[q], on_line(place))
 
     def goes_on(q):
         return ((q < at) & (at + 1 < line)) | ((q > at) & (at > 0))
 
-    def arrived(q, s):
-        return remote(slot(q, s), slot(q, s), ag_send.at[0, q], ag_recv.at[q, s], twin)
-
-    def forward(q):
-        arrived(q, side).wait_recv()
-        to_twin(q).start()
-
-        @pl.when(goes_on(q))
-        def _():
-            onward(q).start()
+    def wait_z(q):
+        remote(slot(q, side), slot(q, side), z_send.at[1, q], z_recv.at[q], twin).wait_recv()
+
+    def wait_y(q, h):
+        view = slot_half(q, 1 - side, h)
+        remote(view, view, y_send.at[q, h], y_recv.at[q, h], twin).wait_recv()
 
     def go_copy(step):
         other = lax.rem(row + step, n_row)
@@ -146,17 +157,27 @@
         view = gp.at[block(g, big), block(which * tiles + j, tile)]
         return remote(view, view, gp_send.at[g, j], gp_recv.at[g, j], mate)
 
+    def swapped(j):
+        return lax.rem(j, 4) == 0
+
+    def by(j, kept, other):
+        return jnp.where(swapped(j), other, kept)
+
+    beside_col, twin_col = beside * PAIR + side, at * PAIR + 1 - side
+
     def pair_copy(g, b, j):
-        return remote(
-            term.at[g, block(b * PAIR + 1 - side, own), block(j, wide)],
+        source = by(j, b * PAIR + 1 - side, (1 - sib) * PAIR + b)
+        return remote(
+            term.at[g, block(source, own), block(j, wide)],
             pair_in.at[g, block(b, own), block(j, wide)],
-            pair_send.at[g, b, j], pair_recv.at[g, b, j], twin,
+            pair_send.at[g, b, j], pair_recv.at[g, b, j], (row, by(j, twin_col, beside_col)),
         )
 
     def sib_copy(g, j):
-        return remote(
-            both.at[g, block(1 - sib, own), block(j, wide)], sib_in.at[g, :, block(j, wide)],
-            sib_send.at[g, j], sib_recv.at[g, j], sibling,
+        source = by(j, 1 - sib, 1 - side)
+        return remote(
+            both.at[g, block(source, own), block(j, wide)], sib_in.at[g, :, block(j, wide)],
+            sib_send.at[g, j], sib_recv.at[g, j], (row, by(j, beside_col, twin_col)),
         )
 
     def line_copy(g, j):
@@ -206,7 +227,7 @@
     pl.semaphore_wait(barrier, line + n_row - 1)
 
     up, down = jnp.minimum(at + 1, line - 1), jnp.maximum(at - 1, 0)
-    own_to(0, twin).start()
+    own_half(1).start()
 
     @pl.when(at + 1 < line)
     def _():
@@ -216,12 +237,23 @@
     def _():
         own_to(2, on_line(down)).start()
 
+    own_half(0).start()
+
     @pl.loop(1, n_row)
     def _(step):
         go_copy(step).start()
 
     x_copy.wait()
-    forward(block_of(group, 1))
+    wait_y(at, 1)
+    twin_to_sibling().start()
+    wait_z(beside)
+    to_twin(beside, 0).start()
+
+    @pl.when(goes_on(beside))
+    def _():
+        onward(beside).start()
+
+    wait_y(at, 0)
 
     def slabs(height, base, width, body):
         @pl.loop(0, height // small)
@@ -245,16 +277,26 @@
         g3 = group_of(jnp.clip(k - 3, 0, groups - 1))
         coming = group_of(jnp.minimum(k + 1, groups - 1))
         more = k + 1 < groups
-        second = block_of(coming, 1)
-
-        @pl.when(more)
-        def _():
-            forward(block_of(coming, 0))
+        first, second = block_of(coming, 0), block_of(coming, 1)
+
+        @pl.when(more & goes_on(first))
+        def _():
+            wait_z(first)
+            onward(first).start()
 
         @pl.when(k < groups)
         def _():
             for i in range(PAIR):
-                arrived(block_of(g, i), 1 - side).wait_recv()
+                @pl.when((k > 0) | (block_of(g, i) != at))
+                def _():
+                    for h in range(2):
+                        wait_y(block_of(g, i), h)
+
+            @pl.when(more & goes_on(first))
+            def _():
+                for h in range(2):
+                    to_twin(first, h).start()
+
             x_copy_out(g).start()
 
             @pl.when(k == 0)
@@ -267,9 +309,18 @@
                 core_copy(g, j).start()
                 product(g, core * tiles + j)
 
+                @pl.when(more & (j == 0) & ~goes_on(first))
+                def _():
+                    wait_z(first)
+                    for h in range(2):
+                        to_twin(first, h).start()
+
                 @pl.when(more & (j == tiles // 2) & goes_on(second))
                 def _():
-                    forward(second)
+                    wait_z(second)
+                    onward(second).start()
+                    for h in range(2):
+                        to_twin(second, h).start()
 
                 core_copy(g, j).wait_recv()
 
@@ -288,7 +339,9 @@
 
             @pl.when(more & ~goes_on(second))
             def _():
-                forward(second)
+                wait_z(second)
+                for h in range(2):
+                    to_twin(second, h).start()
 
         @pl.when((k >= 1) & (k <= groups))
         def _():
@@ -343,7 +396,7 @@
                     pair_copy(g2, b, j).wait_recv()
 
                     def add(top, columns):
-                        mine = term[g2, at_row((b * PAIR + side) * own + top), columns]
+                        mine = term[g2, at_row(by(j, b * PAIR + side, sib * PAIR + b) * own + top), columns]
                         here = at_row(b * own + top)
                         both[g2, here, columns] = (
                             mine.astype(jnp.float32)
@@ -360,7 +413,7 @@
                 sib_copy(g3, j).wait_recv()
 
                 def add(top, columns):
-                    mine = both[g3, at_row(sib * own + top), columns]
+                    mine = both[g3, at_row(by(j, sib, side) * own + top), columns]
                     summed[g3, at_row(top), columns] = (
                         mine.astype(jnp.float32)
                         + sib_in[g3, at_row(top), columns].astype(jnp.float32)
@@ -387,7 +440,9 @@
 
         slabs(own, j, wide, finish)
 
-    own_to(0, twin).wait_send()
+    own_half(0).wait_send()
+    own_half(1).wait_send()
+    twin_to_sibling().wait_send()
 
     @pl.when(at + 1 < line)
     def _():
@@ -405,7 +460,11 @@
     def _(q):
         @pl.when(q != at)
         def _():
-            to_twin(q).wait_send()
+            to_twin(q, 0).wait_send()
+
+        @pl.when((q != at) & (q != beside))
+        def _():
+            to_twin(q, 1).wait_send()
 
         @pl.when(goes_on(q))
         def _():
@@ -478,7 +537,7 @@
             pltpu.VMEM((groups, own, depth), bf16),
             pltpu.VMEM((groups, own, depth), bf16),
             DMA, DMA, DMA, DMA((2, groups)),
-            DMA((line, PAIR)), DMA((3, line)),
+            DMA((line,)), DMA((3, line)), DMA((line, 2)), DMA((line, 2)),
             DMA((n_row,)), DMA((n_row,)),
             DMA((groups, tiles)), DMA((groups, tiles)),
             DMA((groups, chips, tiles)), DMA((groups, chips, tiles)),

time: 135 us -> 124 us (0.919)
  Pallas kernels: 117 us -> 106 us
    pallas_call x1, Pallas kernels: 117 us -> 106 us  [fused(): pl.pallas_call(functools.partial(kernel, n_row, n_col), out_shape=(jax.Sh...]
where the time goes in v3:
time: 124 us
  Pallas kernels  106 us (85%)
  matrix products  16.4 us (13%)
    pallas_call x1, Pallas kernels, fused(): pl.pallas_call(functools.partial(kernel, n_row, n_col), out_shape=(jax.Sh...  106 us
    dot_general x1, matrix products, shards(): lax.dot_general(gathered, grad_pre, (((0,), (0,)), ((), ())), preferred_e...  16.4 us

profile of v3, /device:TPU:0, one launch (start us, length us, event | category | flops | bytes accessed | tf_op | source)
XLA Modules:
  0.0 124.3 jit_solution(12369844670836564400)
XLA Ops:
  0.6 106.5 %shard_map.50 = (bf16[64,3072]{1,0:T(8,128)(2,1)}, bf16[512,3072]{1,0:T(8,128)(2,1)}, bf16[512,3072]{1,0:T(8,128)(2,1)}) custom-call(bf16[64,3072]{1,0:T(8,128)(2,1)} %x_ref.1, bf16[3072,3072]{1,0:T(8,128)(2,1)} %w_ref.1, bf16[128,3072]{1,0:T(8,128)(2,1)} %go_ref.1), custom_call_target="tpu_custom_call" | custom-call | flops 19327352832 | bytes 18874368 | tf_op jit(solution)/shard_map/pallas_call | solution.py:511
  107.1 0.0 copy-start
  107.1 16.4 %convolution_convert_fusion = bf16[3072,3072]{1,0:T(8,128)(2,1)} fusion(bf16[512,3072]{1,0:T(8,128)(2,1)} %get-tuple-element.6, bf16[512,3072]{1,0:T(8,128)(2,1)} %get-tuple-element.7), kind=kOutput, calls=%fused_computation | convolution fusion | flops 9673113600 | bytes 25165824 | tf_op jit(solution)/shard_map/dot_general | solution.py:563
  123.6 0.0 copy-done
  123.6 0.7 copy.6
Async XLA Ops:
  107.1 16.4 %copy-start = (bf16[64,3072]{1,0:T(8,128)(2,1)S(1)}, bf16[64,3072]{1,0:T(8,128)(2,1)}, u32[]{:S(2)}) copy-start(bf16[64,3072]{1,0:T(8,128)(2,1)} %get-tuple-element.10) | copy-start | bytes 1179652

commit v4 on v3

--- a/solution.py
+++ b/solution.py
@@ -555,15 +555,47 @@
     )(inputs, weight, grad_out)
 
 
+def weight_kernel(x_ref, gp_ref, gw_ref, turned):
+    turned[...] = x_ref[...].T
+    width = tile_of(gp_ref.shape[1], 1024)
+
+    @pl.loop(0, gp_ref.shape[1] // width)
+    def _(j):
+        columns = block(j, width)
+        gw_ref[:, columns] = jnp.dot(
+            turned[...], gp_ref[:, columns], preferred_element_type=jnp.float32
+        ).astype(gw_ref.dtype)
+
+
+def weight_gradient(gathered, grad_pre):
+    tokens, depth = gathered.shape
+    units = grad_pre.shape[1]
+    high = tile_of(depth, 512)
+    return pl.pallas_call(
+        weight_kernel,
+        out_shape=jax.ShapeDtypeStruct((depth, units), jnp.bfloat16),
+        grid=(depth // high,),
+        in_specs=[
+            pl.BlockSpec((tokens, high), lambda i: (0, i)),
+            pl.BlockSpec((tokens, units), lambda i: (0, 0)),
+        ],
+        out_specs=pl.BlockSpec((high, units), lambda i: (i, 0)),
+        scratch_shapes=[pltpu.VMEM((high, tokens), jnp.bfloat16)],
+        cost_estimate=pl.CostEstimate(
+            flops=2 * tokens * depth * units,
+            bytes_accessed=2 * (depth * units + tokens * depth + tokens * units),
+            transcendentals=0,
+        ),
+        compiler_params=pltpu.CompilerParams(vmem_limit_bytes=48 * 1024 * 1024),
+    )(gathered, grad_pre)
+
+
 def solution(mesh):
     n_row, n_col = mesh.shape["row"], mesh.shape["col"]
 
     def shards(inputs, weight, grad_out):
         grad_input, gathered, grad_pre = fused(n_row, n_col, inputs, weight, grad_out)
-        grad_weight = lax.dot_general(
-            gathered, grad_pre, (((0,), (0,)), ((), ())), preferred_element_type=jnp.float32
-        )
-        return grad_input, grad_weight.astype(jnp.bfloat16)
+        return grad_input, weight_gradient(gathered, grad_pre)
 
     return jax.shard_map(
         shards,

time: 124 us -> 128 us (1.032)
  Pallas kernels: 106 us -> 124 us
  matrix products: 16.4 us -> 0 us
  local copies, waits for them, and re-layouts: 0.75 us -> 2.63 us
    pallas_call x0 -> x1, Pallas kernels: none -> 17.9 us  [weight_gradient(): pl.pallas_call(weight_kernel, out_shape=jax.ShapeDtypeStruct((depth, unit...]
    dot_general x1 -> x0, matrix products: 16.4 us -> none  [shards(): lax.dot_general(gathered, grad_pre, (((0,), (0,)), ((), ())), preferred_e...]
    unnamed x3 -> x5, local copies, waits for them, and re-layouts: 0.75 us -> 2.63 us
where the time goes in v4:
time: 128 us
  Pallas kernels  124 us (97%)
  local copies, waits for them, and re-layouts  2.63 us (2%)
    pallas_call x1, Pallas kernels, fused(): pl.pallas_call(functools.partial(kernel, n_row, n_col), out_shape=(jax.Sh...  106 us
    pallas_call x1, Pallas kernels, weight_gradient(): pl.pallas_call(weight_kernel, out_shape=jax.ShapeDtypeStruct((depth, unit...  17.9 us
    unnamed x5, local copies, waits for them, and re-layouts  2.63 us

profile of v4, /device:TPU:0, one launch (start us, length us, event | category | flops | bytes accessed | tf_op | source)
XLA Modules:
  0.0 127.6 jit_solution(717776369687825792)
XLA Ops:
  0.6 106.5 %shard_map.50 = (bf16[64,3072]{1,0:T(8,128)(2,1)}, bf16[512,3072]{1,0:T(8,128)(2,1)}, bf16[512,3072]{1,0:T(8,128)(2,1)}) custom-call(bf16[64,3072]{1,0:T(8,128)(2,1)} %x_ref.1, bf16[3072,3072]{1,0:T(8,128)(2,1)} %w_ref.1, bf16[128,3072]{1,0:T(8,128)(2,1)} %go_ref.1), custom_call_target="tpu_custom_call" | custom-call | flops 19327352832 | bytes 18874368 | tf_op jit(solution)/shard_map/pallas_call | solution.py:511
  107.1 0.0 copy-start
  107.1 1.9 %copy-done = bf16[512,3072]{1,0:T(8,128)(2,1)S(1)} copy-done((bf16[512,3072]{1,0:T(8,128)(2,1)S(1)}, bf16[512,3072]{1,0:T(8,128)(2,1)}, u32[]{:S(2)}) %copy-start) | copy-done | bytes 3145752
  109.0 0.0 copy-start.1
  109.0 17.9 %shard_map.51 = bf16[3072,3072]{1,0:T(8,128)(2,1)} custom-call(bf16[512,3072]{1,0:T(8,128)(2,1)S(1)} %copy-done, bf16[512,3072]{1,0:T(8,128)(2,1)} %get-tuple-element.7.gp_ref), custom_call_target="tpu_custom_call" | custom-call | flops 9663676416 | bytes 25165824 | tf_op jit(solution)/shard_map/pallas_call | solution.py:574
  126.9 0.0 copy-done.1
  126.9 0.7 copy.6
Async XLA Ops:
  107.1 1.9 %copy-start = (bf16[512,3072]{1,0:T(8,128)(2,1)S(1)}, bf16[512,3072]{1,0:T(8,128)(2,1)}, u32[]{:S(2)}) copy-start(bf16[512,3072]{1,0:T(8,128)(2,1)} %get-tuple-element.6.x_ref) | copy-start | bytes 9437188
  109.0 17.9 %copy-start.1 = (bf16[64,3072]{1,0:T(8,128)(2,1)S(1)}, bf16[64,3072]{1,0:T(8,128)(2,1)}, u32[]{:S(2)}) copy-start(bf16[64,3072]{1,0:T(8,128)(2,1)} %get-tuple-element.10) | copy-start | bytes 1179652

commit v5 on v3

--- a/solution.py
+++ b/solution.py
@@ -269,12 +269,11 @@
             xs_all[block(g, big), :], w[:, columns], preferred_element_type=jnp.float32
         ).astype(part.dtype)
 
-    @pl.loop(0, groups + 3)
+    @pl.loop(0, groups + 2)
     def _(k):
         g = group_of(jnp.minimum(k, groups - 1))
         g1 = group_of(jnp.clip(k - 1, 0, groups - 1))
         g2 = group_of(jnp.clip(k - 2, 0, groups - 1))
-        g3 = group_of(jnp.clip(k - 3, 0, groups - 1))
         coming = group_of(jnp.minimum(k + 1, groups - 1))
         more = k + 1 < groups
         first, second = block_of(coming, 0), block_of(coming, 1)
@@ -388,42 +387,45 @@
                 for b in range(PAIR):
                     pair_copy(g1, b, j).start()
 
-        @pl.when((k >= 2) & (k <= groups + 1))
-        def _():
-            @pl.loop(0, pieces)
-            def _(j):
-                for b in range(PAIR):
-                    pair_copy(g2, b, j).wait_recv()
+        @pl.when(k >= 2)
+        def _():
+            @pl.loop(0, pieces + 1)
+            def _(step):
+                @pl.when(step < pieces)
+                def _():
+                    j = jnp.minimum(step, pieces - 1)
+                    for b in range(PAIR):
+                        pair_copy(g2, b, j).wait_recv()
+
+                        def add(top, columns):
+                            start = by(j, b * PAIR + side, sib * PAIR + b) * own
+                            mine = term[g2, at_row(start + top), columns]
+                            here = at_row(b * own + top)
+                            both[g2, here, columns] = (
+                                mine.astype(jnp.float32)
+                                + pair_in[g2, here, columns].astype(jnp.float32)
+                            ).astype(both.dtype)
+
+                        slabs(own, j, wide, add)
+                    sib_copy(g2, j).start()
+
+                @pl.when(step >= 1)
+                def _():
+                    j = jnp.maximum(step - 1, 0)
+                    sib_copy(g2, j).wait_recv()
 
                     def add(top, columns):
-                        mine = term[g2, at_row(by(j, b * PAIR + side, sib * PAIR + b) * own + top), columns]
-                        here = at_row(b * own + top)
-                        both[g2, here, columns] = (
+                        mine = both[g2, at_row(by(j, sib, side) * own + top), columns]
+                        summed[g2, at_row(top), columns] = (
                             mine.astype(jnp.float32)
-                            + pair_in[g2, here, columns].astype(jnp.float32)
-                        ).astype(both.dtype)
+                            + sib_in[g2, at_row(top), columns].astype(jnp.float32)
+                        ).astype(summed.dtype)
 
                     slabs(own, j, wide, add)
-                sib_copy(g2, j).start()
-
-        @pl.when(k >= 3)
-        def _():
-            @pl.loop(0, pieces)
-            def _(j):
-                sib_copy(g3, j).wait_recv()
-
-                def add(top, columns):
-                    mine = both[g3, at_row(by(j, sib, side) * own + top), columns]
-                    summed[g3, at_row(top), columns] = (
-                        mine.astype(jnp.float32)
-                        + sib_in[g3, at_row(top), columns].astype(jnp.float32)
-                    ).astype(summed.dtype)
-
-                slabs(own, j, wide, add)
-
-                @pl.when(g3 != group)
-                def _():
-                    line_copy(g3, j).start()
+
+                    @pl.when(g2 != group)
+                    def _():
+                        line_copy(g2, j).start()
 
     @pl.loop(0, pieces)
     def _(j):

time: 124 us -> 137 us (1.10)
  Pallas kernels: 106 us -> 119 us
    pallas_call x1, Pallas kernels: 106 us -> 119 us  [fused(): pl.pallas_call(functools.partial(kernel, n_row, n_col), out_shape=(jax.Sh...]
where the time goes in v5:
time: 137 us; the launch traced here: 136 us
  Pallas kernels  119 us (87%)
  matrix products  16.4 us (12%)
    pallas_call x1, Pallas kernels, fused(): pl.pallas_call(functools.partial(kernel, n_row, n_col), out_shape=(jax.Sh...  119 us
    dot_general x1, matrix products, shards(): lax.dot_general(gathered, grad_pre, (((0,), (0,)), ((), ())), preferred_e...  16.4 us

profile of v5, /device:TPU:0, one launch (start us, length us, event | category | flops | bytes accessed | tf_op | source)
XLA Modules:
  0.0 136.4 jit_solution(10749612760557108637)
XLA Ops:
  0.6 118.6 %shard_map.50 = (bf16[64,3072]{1,0:T(8,128)(2,1)}, bf16[512,3072]{1,0:T(8,128)(2,1)}, bf16[512,3072]{1,0:T(8,128)(2,1)}) custom-call(bf16[64,3072]{1,0:T(8,128)(2,1)} %x_ref.1, bf16[3072,3072]{1,0:T(8,128)(2,1)} %w_ref.1, bf16[128,3072]{1,0:T(8,128)(2,1)} %go_ref.1), custom_call_target="tpu_custom_call" | custom-call | flops 19327352832 | bytes 18874368 | tf_op jit(solution)/shard_map/pallas_call | solution.py:513
  119.2 0.0 copy-start
  119.3 16.4 %convolution_convert_fusion = bf16[3072,3072]{1,0:T(8,128)(2,1)} fusion(bf16[512,3072]{1,0:T(8,128)(2,1)} %get-tuple-element.6, bf16[512,3072]{1,0:T(8,128)(2,1)} %get-tuple-element.7), kind=kOutput, calls=%fused_computation | convolution fusion | flops 9673113600 | bytes 25165824 | tf_op jit(solution)/shard_map/dot_general | solution.py:565
  135.7 0.0 copy-done
  135.7 0.7 copy.6
Async XLA Ops:
  119.2 16.4 %copy-start = (bf16[64,3072]{1,0:T(8,128)(2,1)S(1)}, bf16[64,3072]{1,0:T(8,128)(2,1)}, u32[]{:S(2)}) copy-start(bf16[64,3072]{1,0:T(8,128)(2,1)} %get-tuple-element.10) | copy-start | bytes 1179652
